TPU v7x, 32 devices: a whole 2x2x4 slice. The times are simulated.
32 devices in a mesh: blk: 4 (over z), head: 8 (over y, x, core).
Axes of the slice: x: 2, y: 2, z: 4, core: 2. Of those that a mesh axis runs over, the one named last changes fastest.
Arguments:
- latent: float32 [64, 256, 256], P('blk', 'head'), may hold values from -6 to 6
- local_gain: float32 [256], replicated, may hold values from 0.5 to 1.5
- local_project: float32 [256, 768], replicated, may hold values from -0.375 to 0.375
- local_output: float32 [256, 256], replicated, may hold values from -0.375 to 0.375
- local_scale: float32 [4], replicated, may hold values from 2 to 500
- merge_first: float32 [1024, 384], replicated, may hold values from -0.1875 to 0.1875
- merge_second: float32 [1536, 512], replicated, may hold values from -0.15625 to 0.15625
- global_gain: float32 [512], replicated, may hold values from 0.5 to 1.5
- global_project: float32 [512, 1536], replicated, may hold values from -0.25 to 0.25
- global_output: float32 [512, 512], replicated, may hold values from -0.25 to 0.25
- global_scale: float32 [8], replicated, may hold values from 2 to 500
- split_second: float32 [512, 1536], replicated, may hold values from -0.25 to 0.25
- split_first: float32 [384, 1024], replicated, may hold values from -0.3125 to 0.3125
Outputs:
- refined: float32 [64, 256, 256], P('blk', 'head')
All inputs are finite; a program needn't handle non-finite values.
Results may differ from a plain program's by a relative error of at most 0.0003.
Values sent between devices are 32-bit elements; how exact they have to be, the bound alone decides.
A program may use at most 128 MiB of HBM per device.

v0:
```python
import functools
import math

import jax
import jax.numpy as jnp
from jax import lax
from jax.experimental import pallas as pl
from jax.experimental.pallas import tpu as pltpu
from jax.sharding import PartitionSpec as P

C0 = 256
HEAD0 = 64
CM = 384
HEADS_G = 8
HEAD_G = 64


EPSILON = 1e-06
FLOOR_VALUE = 0.5
PRECISE = lax.Precision.HIGHEST


def matmul(left, right):
    return jnp.dot(left, right, precision=PRECISE, preferred_element_type=jnp.float32)


def rms_scale(values, gains):
    return values * lax.rsqrt(jnp.mean(values * values, axis=-1, keepdims=True) + EPSILON) * gains


def unit_rows(values):
    return values * lax.rsqrt(jnp.mean(values * values, axis=-1, keepdims=True) + EPSILON)


def floor_rows(values):
    return values * lax.rsqrt(
        jnp.maximum(jnp.mean(values * values, axis=-1, keepdims=True), FLOOR_VALUE)
    )


def split_cells(grid_in, channels):
    grid_rows, grid_cols = (grid_in.shape[0], grid_in.shape[1])
    moved = grid_in.reshape(grid_rows, grid_cols, 2, 2, channels).transpose(0, 2, 1, 3, 4)
    return moved.reshape(2 * grid_rows, 2 * grid_cols, channels)


MESH = pl.DeviceIdType.MESH
HALO = 3
EDGE = 8
LANES = 128
LOG2E = math.log2(math.e)
DIRECTIONS = ((-1, 0), (1, 0), (0, -1), (0, 1), (-1, -1), (-1, 1), (1, -1), (1, 1))


def halves(values):
    high = values.astype(jnp.bfloat16)
    return high, (values - high.astype(jnp.float32)).astype(jnp.bfloat16)


def plain_dot(left, right):
    return jnp.dot(left, right, preferred_element_type=jnp.float32)


def split_dot(left, right):
    left_high, left_low = halves(left)
    right_high, right_low = halves(right)
    return (
        plain_dot(left_low, right_high)
        + plain_dot(left_high, right_low)
        + plain_dot(left_high, right_high)
    )


def group_matrix(width, group):
    rows = lax.broadcasted_iota(jnp.int32, (width, width), 0) // group
    cols = lax.broadcasted_iota(jnp.int32, (width, width), 1) // group
    return jnp.where(rows == cols, 1.0 / group, 0.0).astype(jnp.bfloat16)


def group_mean_squares(values, group):
    high, low = halves(values * values)
    matrix = group_matrix(values.shape[1], group)
    return plain_dot(high, matrix) + plain_dot(low, matrix)


def neighbours(sizes):
    blk, head = lax.axis_index("blk"), lax.axis_index("head")
    for dz, dc in DIRECTIONS:
        row, col = blk + dz, head + dc
        back_row, back_col = blk - dz, head - dc
        there = (row >= 0) & (row < sizes[0]) & (col >= 0) & (col < sizes[1])
        back = (back_row >= 0) & (back_row < sizes[0]) & (back_col >= 0) & (back_col < sizes[1])
        yield (row, col), there, back


def local_kernel(
    sizes,
    latent_ref,
    gain_ref,
    project_ref,
    output_ref,
    scale_ref,
    merge_first_ref,
    merge_second_ref,
    global_gain_ref,
    zero_ref,
    one_ref,
    two_ref,
    normed_ref,
    up_ref,
    down_ref,
    left_ref,
    right_ref,
    query_ref,
    key_ref,
    high_ref,
    low_ref,
    attended_ref,
    zero_chunks,
    one_chunks,
    send_sem,
    recv_sem,
):
    rows, cols, width = latent_ref.shape
    heads = width // HEAD0
    span = cols + EDGE
    low_row, low_col = rows - HALO, cols - EDGE
    blk, head = lax.axis_index("blk"), lax.axis_index("head")
    barrier = pltpu.get_barrier_semaphore()
    count = jnp.int32(0)
    for device, there, back in neighbours(sizes):
        count = count + there.astype(jnp.int32)

        @pl.when(there)
        def _(device=device):
            pl.semaphore_signal(barrier, inc=1, device_id=device, device_id_type=MESH)

    pl.semaphore_wait(barrier, count)

    sources = {-1: slice(0, HALO), 1: slice(low_row, rows)}
    corner_rows = {-1: slice(rows + HALO, rows + 2 * HALO), 1: slice(0, HALO)}
    columns = {-1: slice(0, EDGE), 1: slice(low_col, cols)}

    def copy_of(index, device):
        dz, dc = DIRECTIONS[index]
        if dc == 0:
            source = latent_ref.at[sources[dz]]
            target = down_ref if dz < 0 else up_ref
        else:
            side = right_ref if dc < 0 else left_ref
            if dz == 0:
                source = latent_ref.at[:, columns[dc]]
                target = side.at[HALO : HALO + rows]
            else:
                source = latent_ref.at[sources[dz], columns[dc]]
                target = side.at[corner_rows[dz]]
        return pltpu.make_async_remote_copy(
            src_ref=source,
            dst_ref=target,
            send_sem=send_sem.at[index],
            recv_sem=recv_sem.at[index],
            device_id=device,
            device_id_type=MESH,
        )

    for index, (device, there, back) in enumerate(neighbours(sizes)):

        @pl.when(there)
        def _(index=index, device=device):
            copy_of(index, device).start()

    gain = gain_ref[...]
    head_factor = jnp.concatenate(
        [jnp.full((1, HEAD0), scale_ref[0, h] * (LOG2E / HEAD0), jnp.float32) for h in range(heads)],
        axis=1,
    )
    latent = latent_ref[...].reshape(rows * cols, width)
    normed = rms_scale(latent, gain)
    queries = split_dot(normed, project_ref[:, :width])
    queries = queries * lax.rsqrt(group_mean_squares(queries, HEAD0) + EPSILON) * head_factor
    high, low = halves(queries)
    for h in range(heads):
        a, b = high[:, h * HEAD0 : (h + 1) * HEAD0], low[:, h * HEAD0 : (h + 1) * HEAD0]
        query_ref[h] = jnp.concatenate([a, a, b, b], axis=1)

    for index, (device, there, back) in enumerate(neighbours(sizes)):

        @pl.when(back)
        def _(index=index, device=device):
            copy_of(index, device).wait_recv()

        @pl.when(there)
        def _(index=index, device=device):
            copy_of(index, device).wait_send()

    has_up, has_down = blk > 0, blk < sizes[0] - 1
    has_left, has_right = head > 0, head < sizes[1] - 1
    middle = jnp.concatenate(
        [
            jnp.where(has_up, up_ref[...], 0.0),
            latent_ref[...],
            jnp.where(has_down, down_ref[...], 0.0),
        ],
        axis=0,
    )
    shape = (rows + 2 * HALO, EDGE, width)
    spot = lax.broadcasted_iota(jnp.int32, shape, 1)
    layer = lax.broadcasted_iota(jnp.int32, shape, 0)
    row_there = (has_up | (layer >= HALO)) & (has_down | (layer < rows + HALO))
    side = jnp.where(
        (spot < HALO) & has_right & row_there,
        right_ref[...],
        jnp.where((spot >= EDGE - HALO) & has_left & row_there, left_ref[...], 0.0),
    )
    padded_rows = rows + 2 * HALO
    total = padded_rows * span
    everything = jnp.concatenate([middle, side], axis=1).reshape(total, width)
    keyvals = split_dot(rms_scale(everything, gain), project_ref[:, width:])
    keys = keyvals[:, :width]
    keys = keys * lax.rsqrt(group_mean_squares(keys, HEAD0) + EPSILON)
    high, low = halves(keys)
    value_high, value_low = halves(keyvals[:, width:])
    for h in range(heads):
        part = slice(h * HEAD0, (h + 1) * HEAD0)
        a, b = high[:, part], low[:, part]
        key_ref[h] = jnp.concatenate([a, b, a, b], axis=1)
        high_ref[h] = jnp.concatenate([value_high[:, part], value_low[:, part]], axis=1)
        low_ref[h] = value_high[:, part]

    step_rows = 4
    block = step_rows * cols
    reach = (step_rows + 2 * HALO) * span
    query_at = lax.broadcasted_iota(jnp.int32, (block, 1), 0)
    key_at = lax.broadcasted_iota(jnp.int32, (1, reach), 1)
    query_row, query_col = query_at // cols, query_at % cols
    key_row, place = key_at // span, key_at % span
    key_col = jnp.where(
        place < cols + HALO,
        place,
        jnp.where(place >= span - HALO, place - span, -4 * span),
    )
    col_here = (
        (key_col + head * cols >= 0)
        & (key_col + head * cols < sizes[1] * cols)
    )
    key_col = jnp.where(col_here, key_col, -4 * span)
    row_gap, col_gap = key_row - query_row, key_col - query_col
    near = (row_gap >= 0) & (row_gap <= 2 * HALO) & (col_gap >= -HALO) & (col_gap <= HALO)
    near_bias = jnp.where(near, 0.0, -1e30)

    def attend(step, unused):
        grid_row = blk * rows + step * step_rows - HALO + key_row
        bias = near_bias + jnp.where(
            (grid_row >= 0) & (grid_row < sizes[0] * rows), 0.0, -1e30
        )
        queries_at = pl.ds(pl.multiple_of(step * block, block), block)
        keys_at = pl.ds(pl.multiple_of(step * step_rows * span, step_rows * span), reach)
        parts = []
        for h in range(heads):
            scores = (
                lax.dot_general(
                    query_ref[h, queries_at],
                    key_ref[h, keys_at],
                    (((1,), (1,)), ((), ())),
                    preferred_element_type=jnp.float32,
                )
                + bias
            )
            weights = jnp.exp2(scores - jnp.max(scores, axis=1, keepdims=True))
            weight_sum = jnp.sum(weights, axis=1, keepdims=True)
            weight_high, weight_low = halves(weights)
            wide = plain_dot(weight_high, high_ref[h, keys_at])
            mixture = (
                wide[:, :HEAD0]
                + wide[:, HEAD0:]
                + plain_dot(weight_low, low_ref[h, keys_at])
            )
            parts.append(mixture / weight_sum)
        attended_ref[queries_at] = jnp.concatenate(parts, axis=1)
        return unused

    lax.fori_loop(0, rows // step_rows, attend, 0)
    zero = latent + split_dot(attended_ref[...], output_ref[...])
    zero_ref[...] = zero
    store_chunks(zero_chunks, zero)
    merged = merge_from(zero_chunks, rows, cols)
    one = split_dot(merged, merge_first_ref[...])
    one_ref[...] = one
    store_chunks(one_chunks, one)
    merged = merge_from(one_chunks, rows // 2, cols // 2)
    two = split_dot(merged, merge_second_ref[...])
    two_ref[...] = two
    normed_ref[...] = rms_scale(two, global_gain_ref[...])


def store_chunks(ref, values):
    for chunk in range(ref.shape[0]):
        ref[chunk] = values[:, chunk * LANES : (chunk + 1) * LANES]


def merge_from(ref, rows, cols):
    cells, width = rows * cols, ref.shape[0] * LANES
    evens, odds = (
        jnp.concatenate(
            [
                ref[chunk, pl.ds(start, cells // 2, stride=2)]
                for chunk in range(ref.shape[0])
            ],
            axis=1,
        ).reshape(rows // 2, 2, cols // 2, width)
        for start in (0, 1)
    )
    pieces = [
        source[:, which].reshape(cells // 4, width)
        for which in (0, 1)
        for source in (evens, odds)
    ]
    return jnp.concatenate(pieces, axis=1)


def local_part(latent, gain, project, output, scale, merge_first, merge_second, global_gain):
    rows, cols, width = latent.shape
    sizes = (lax.axis_size("blk"), lax.axis_size("head"))
    heads = width // HEAD0
    total = (rows + 2 * HALO) * (cols + EDGE)
    vmem = pl.BlockSpec(memory_space=pltpu.VMEM)
    mid, coarse = merge_first.shape[1], merge_second.shape[1]
    f32, b16 = jnp.float32, jnp.bfloat16
    return pl.pallas_call(
        functools.partial(local_kernel, sizes),
        out_shape=[
            jax.ShapeDtypeStruct((rows * cols, width), f32),
            jax.ShapeDtypeStruct((rows * cols // 4, mid), f32),
            jax.ShapeDtypeStruct((rows * cols // 16, coarse), f32),
            jax.ShapeDtypeStruct((rows * cols // 16, coarse), f32),
        ],
        in_specs=[vmem] * 4 + [pl.BlockSpec(memory_space=pltpu.SMEM)] + [vmem] * 3,
        out_specs=[vmem] * 4,
        scratch_shapes=[
            pltpu.VMEM((HALO, cols, width), f32),
            pltpu.VMEM((HALO, cols, width), f32),
            pltpu.VMEM((rows + 2 * HALO, EDGE, width), f32),
            pltpu.VMEM((rows + 2 * HALO, EDGE, width), f32),
            pltpu.VMEM((heads, rows * cols, 4 * HEAD0), b16),
            pltpu.VMEM((heads, total, 4 * HEAD0), b16),
            pltpu.VMEM((heads, total, 2 * HEAD0), b16),
            pltpu.VMEM((heads, total, HEAD0), b16),
            pltpu.VMEM((rows * cols, width), f32),
            pltpu.VMEM((width // LANES, rows * cols, LANES), f32),
            pltpu.VMEM((mid // LANES, rows * cols // 4, LANES), f32),
            pltpu.SemaphoreType.DMA((8,)),
            pltpu.SemaphoreType.DMA((8,)),
        ],
        compiler_params=pltpu.CompilerParams(
            collective_id=0, has_side_effects=True, vmem_limit_bytes=48 * 2**20
        ),
        name="local_part",
    )(
        latent,
        gain[None],
        project,
        output,
        scale[None],
        merge_first,
        merge_second,
        global_gain[None],
    )


def shards(
    latent,
    local_gain,
    local_project,
    local_output,
    local_scale,
    merge_first,
    merge_second,
    global_gain,
    global_project,
    global_output,
    global_scale,
    split_second,
    split_first,
):
    tile_rows, tile_cols = (latent.shape[0], latent.shape[1])
    level_zero, level_one, level_two, normed_two = local_part(
        latent,
        local_gain,
        local_project,
        local_output,
        local_scale,
        merge_first,
        merge_second,
        global_gain,
    )
    level_zero = level_zero.reshape(tile_rows, tile_cols, C0)
    level_one = level_one.reshape(tile_rows // 2, tile_cols // 2, CM)
    own_tokens = level_two.shape[0]
    group_size = lax.axis_size("head")
    copies = group_size // HEADS_G
    position = lax.axis_index("head")
    head_id = position // copies
    part_id = position % copies
    span = HEADS_G * own_tokens
    own_project = lax.dynamic_slice_in_dim(global_project, head_id * 3 * HEAD_G, 3 * HEAD_G, 1)
    projected = matmul(lax.all_gather(normed_two, "head", axis=0, tiled=True), own_project)
    projected = projected.reshape(-1, 1, 3, HEAD_G)
    query_part = lax.dynamic_slice_in_dim(projected[:, :, 0], part_id * span, span, 0)
    global_queries = floor_rows(query_part)
    global_keys = floor_rows(projected[:, :, 1])
    global_values = projected[:, :, 2]
    own_scale = lax.dynamic_slice_in_dim(global_scale, head_id, 1, 0)
    factor = own_scale / HEAD_G
    query_count = global_queries.shape[0]
    starting = (
        jnp.full((1, query_count), -jnp.inf, jnp.float32),
        jnp.zeros((1, query_count), jnp.float32),
        jnp.zeros((1, query_count, HEAD_G), jnp.float32),
    )
    running = starting
    key_piece = lax.all_gather(global_keys, "blk", axis=0, tiled=True)
    value_piece = lax.all_gather(global_values, "blk", axis=0, tiled=True)
    piece_rows = key_piece.shape[0]
    block_rows = math.gcd(piece_rows, 2048)
    key_blocks = key_piece.reshape(piece_rows // block_rows, block_rows, 1, HEAD_G)
    value_blocks = value_piece.reshape(piece_rows // block_rows, block_rows, 1, HEAD_G)

    def advance(current, blocks_now):
        key_block, value_block = blocks_now
        best_score, weight_sum, accumulated = current
        scores = (
            jnp.einsum(
                "qhd,khd->hqk",
                global_queries,
                key_block,
                precision=PRECISE,
                preferred_element_type=jnp.float32,
            )
            * factor[:, None, None]
        )
        raised_best = jnp.maximum(best_score, jnp.max(scores, axis=2))
        rescale = jnp.exp(best_score - raised_best)
        weights = jnp.exp(scores - raised_best[:, :, None])
        weight_sum = weight_sum * rescale + jnp.sum(weights, axis=2)
        accumulated = accumulated * rescale[:, :, None] + jnp.einsum(
            "hqk,khd->hqd",
            weights,
            value_block,
            precision=PRECISE,
            preferred_element_type=jnp.float32,
        )
        return ((raised_best, weight_sum, accumulated), None)

    running, unused = lax.scan(advance, running, (key_blocks, value_blocks))
    best_score, weight_sum, accumulated = running
    attention_out = (accumulated / weight_sum[:, :, None])[0]
    placed = lax.dynamic_update_slice_in_dim(
        jnp.zeros((group_size * own_tokens, HEAD_G), jnp.float32), attention_out, part_id * span, 0
    )
    own_output = lax.dynamic_slice_in_dim(global_output, head_id * HEAD_G, HEAD_G, 0)
    mixed_global = lax.psum_scatter(
        matmul(placed, own_output), "head", scatter_dimension=0, tiled=True
    )
    global_mixed = level_two + mixed_global
    up_one = (
        split_cells(
            matmul(global_mixed, split_second).reshape(tile_rows // 4, tile_cols // 4, 4 * CM), CM
        )
        + level_one
    )
    refined = (
        split_cells(
            matmul(up_one.reshape(-1, CM), split_first).reshape(
                tile_rows // 2, tile_cols // 2, 4 * C0
            ),
            C0,
        )
        + level_zero
    )
    return refined


def solution(mesh):
    in_specs = (P("blk", "head", None), P(), P(), P(), P(), P(), P(), P(), P(), P(), P(), P(), P())
    out_specs = P("blk", "head", None)
    return jax.shard_map(shards, mesh=mesh, in_specs=in_specs, out_specs=out_specs, check_vma=False)
```

profile of v0, /device:TPU:0, one launch (start us, length us, event | category | flops | bytes accessed | tf_op | source)
XLA Modules:
  0.0 145.0 jit_solution(948765177098490050)
XLA Ops:
  6.5 0.0 copy-start
  6.5 0.0 reduce-scatter.2.cloned.1.call-start
  6.5 0.0 copy-start.1
  6.5 1.6 %copy-done.1 = f32[1024,384]{1,0:T(8,128)S(1)} copy-done((f32[1024,384]{1,0:T(8,128)S(1)}, f32[1024,384]{1,0:T(8,128)}, u32[]{:S(2)}) %copy-start.1) | copy-done | bytes 1572888
  8.1 0.0 copy-start.2
  8.1 1.1 copy-done.2
  9.2 0.0 copy-start.3
  9.2 1.0 copy-done.3
  10.3 0.0 copy-start.5
  10.3 0.9 copy-done.5
  11.2 0.0 copy-start.6
  11.2 0.7 copy-done.6
  11.9 0.0 copy-start.7
  11.9 0.7 copy-done.7
  12.6 0.0 copy-start.8
  12.6 0.7 copy-done.8
  13.2 0.0 copy-start.11
  13.2 21.5 %local_part.1 = (f32[512,256]{1,0:T(8,128)S(1)}, f32[128,384]{1,0:T(8,128)S(1)}, f32[32,512]{1,0:T(8,128)S(1)}, f32[32,512]{1,0:T(8,128)S(1)}) custom-call(f32[16,32,256]{2,1,0:T(8,128)S(1)} %copy-done.3, f32[1,256]{1,0:T(1,128)S(1)} %bitcast.47, f32[256,768]{1,0:T(8,128)S(1)} %copy-done.2, f32[256,256]{1,0:T(8,128)S(1)} %copy-done.5, f32[1,4]{1,0:T(1,128)S(1)} %bitcast.48, ...), custom_call_target="tpu_custom_call" | custom-call | tf_op jit(solution)/shard_map/local_part/pallas_call | solution.py:329
  34.7 0.0 copy-start.4
  34.7 0.8 copy-done.4
  35.5 12.2 %all_gather.9 = f32[256,512]{1,0:T(8,128)} all-gather(f32[32,512]{1,0:T(8,128)S(1)} %get-tuple-element.32), channel_id=1, replica_groups=mesh['blk'=4,'head'=8] {'head'}, dimensions={0}, use_global_device_ids=true | all-gather | bytes 589824 | tf_op jit(solution)/shard_map/all_gather | solution.py:406
  47.7 0.0 copy-done
  47.7 2.2 %fusion.3 = f32[256,192]{0,1:T(8,128)S(1)} fusion(f32[256,512]{1,0:T(8,128)} %all_gather.9, f32[512,1536]{1,0:T(8,128)S(1)} %copy-done, s32[]{:T(128)S(6)} %select_n.18), kind=kOutput, calls=%fused_computation.7 | convolution fusion | flops 301989888 | bytes 1245188 | tf_op jit(solution)/shard_map/dot_general | solution.py:24
  49.9 0.0 copy-start.10
  50.0 0.6 copy-done.10
  50.6 0.9 fusion.13
  51.5 14.6 %all-gather = f32[1024,1,1,64]{0,3,2,1:T(8,128)} all-gather(f32[256,1,1,64]{0,3,2,1:T(8,128)S(1)} %get-tuple-element.37), channel_id=2, replica_groups=mesh['blk'=4,'head'=8] {'blk'}, dimensions={0}, use_global_device_ids=true | all-gather | bytes 327680 | tf_op jit(solution)/shard_map/all_gather | solution.py:422
  66.1 15.4 %all_gather.10 = f32[1024,1,64]{0,2,1:T(8,128)} all-gather(f32[256,1,64]{0,2,1:T(8,128)S(1)} %fusion.13), channel_id=1, replica_groups=mesh['blk'=4,'head'=8] {'blk'}, dimensions={0}, use_global_device_ids=true | all-gather | bytes 327680 | tf_op jit(solution)/shard_map/all_gather | solution.py:421
  81.5 0.0 copy-done.11
  81.5 0.6 dynamic_slice.16
  82.7 2.1 %fusion.20 = (f32[256]{0:T(256)S(1)}, f32[256,1024]{1,0:T(8,128)S(1)}) fusion(f32[]{:T(128)} %bitcast.7, f32[1024,1,64]{0,2,1:T(8,128)} %all_gather.10, f32[256,1,3,64]{0,3,2,1:T(8,128)} %bitcast.54, f32[256]{0:T(256)S(1)} %maximum_rsqrt_fusion.1), kind=kOutput, calls=%fused_computation.31 | convolution fusion | flops 201867008 | bytes 1378816 | tf_op jit(solution)/shard_map/while/body/eval_jaxpr/qhd,khd->hqk/dot_general | solution.py:432
  84.8 0.0 copy-start.9
  84.8 1.0 copy-done.9
  85.8 0.3 fusion.1
  86.1 2.3 %fusion = f32[256,64]{1,0:T(8,128)S(1)} fusion(f32[256,1024]{1,0:T(8,128)} %copy-done.9, f32[256]{0:T(256)S(1)} %get-tuple-element.41, f32[1024,1,1,64]{0,3,2,1:T(8,128)} %all-gather, f32[256]{0:T(256)S(1)} %get-tuple-element.40, f32[256]{0:T(256)S(1)} %get-tuple-element.39), kind=kOutput, calls=%fused_computation.3 | convolution fusion | flops 201621504 | bytes 1379328 | tf_op jit(solution)/shard_map/while/body/eval_jaxpr/hqk,khd->hqd/dot_general | solution.py:445
  88.4 2.3 %fusion.7 = f32[256,512]{1,0:T(8,128)} fusion(f32[256,64]{1,0:T(8,128)S(1)} %fusion, f32[512,512]{1,0:T(8,128)} %param.22, s32[]{:T(128)S(6)} %select_n.20), kind=kOutput, calls=%fused_computation.12 | convolution fusion | flops 100663296 | bytes 720900 | tf_op jit(solution)/shard_map/dot_general | solution.py:24
  90.7 0.0 reduce-scatter.2.cloned.1.call-update
  90.7 3.0 %copy.20 = f32[1024,384]{1,0:T(8,128)} copy(f32[1024,384]{0,1:T(8,128)} %bitcast.50) | data formatting | bytes 3145728 | tf_op jit(solution)/shard_map/dot_general | solution.py:24
  93.7 30.0 %reduce-scatter.2.cloned.1.call-done = f32[32,512]{1,0:T(8,128)} async-done(((f32[256,512]{1,0:T(8,128)}), f32[32,512]{1,0:T(8,128)}) %reduce-scatter.2.cloned.1.call-update) | async-done | bytes 65552 | tf_op jit(solution)/shard_map/reduce_scatter | solution.py:461
  123.8 3.8 %fusion.10 = f32[32,1536]{1,0:T(8,128)S(1)} fusion(f32[512,1536]{1,0:T(8,128)} %param.24, f32[32,512]{1,0:T(8,128)S(1)} %get-tuple-element.23, f32[32,512]{1,0:T(8,128)} %reduce-scatter.2.cloned.1.call-done), kind=kOutput, calls=%fused_computation.16 | convolution fusion | flops 302006272 | bytes 3473408 | tf_op jit(solution)/shard_map/dot_general | solution.py:24
  127.6 0.1 copy.22
  127.7 0.8 reshape.171
  128.5 0.9 add.49
  129.5 3.1 %convolution_bitcast_fusion = f32[8,2,16,2,256]{4,2,3,1,0:T(8,128)S(1)} fusion(f32[8,16,384,1,1]{2,1,4,3,0:T(8,128)S(1)} %bitcast.55, f32[2,2,256,384,1]{3,2,1,0,4:T(8,128)} %bitcast.49), kind=kOutput, calls=%fused_computation.1 | convolution fusion | flops 603979776 | bytes 2293760 | tf_op jit(solution)/shard_map/dot_general | solution.py:24
  132.6 1.2 copy.18
  133.8 2.2 %reshape.172 = f32[16,32,256]{2,1,0:T(8,128)} reshape(f32[8,2,16,2,256]{4,3,2,1,0:T(2,128)} %copy.18) | data formatting | bytes 1048576 | tf_op jit(solution)/shard_map/reshape | solution.py:44
  136.0 2.1 %add.50 = f32[16,32,256]{2,1,0:T(8,128)} add(f32[16,32,256]{2,1,0:T(8,128)} %reshape.172, f32[16,32,256]{2,1,0:T(8,128)} %bitcast.45) | non-fusion elementwise | flops 131072 | bytes 1572864 | tf_op jit(solution)/shard_map/add | solution.py:472
  (5 shorter events, 0.1 us)
Async XLA Ops:
  6.5 41.2 %copy-start = (f32[512,1536]{1,0:T(8,128)S(1)}, f32[512,1536]{1,0:T(8,128)}, u32[]{:S(2)}) copy-start(f32[512,1536]{1,0:T(8,128)} %param.21) | copy-start | bytes 9437188
  6.5 117.3 %reduce-scatter.2.cloned.1.call-start = ((), (), s32[]{:S(2)}) async-start(), calls=%async_computation.1 | async-start | bytes 589824 | tf_op jit(solution)/shard_map/reduce_scatter | solution.py:461
  6.5 1.6 %copy-start.1 = (f32[1024,384]{1,0:T(8,128)S(1)}, f32[1024,384]{1,0:T(8,128)}, u32[]{:S(2)}) copy-start(f32[1024,384]{1,0:T(8,128)} %merge_first_ref.1) | copy-start | bytes 4718596
  8.1 1.1 copy-start.2
  9.2 1.0 copy-start.3
  10.3 0.9 copy-start.5
  11.2 0.7 copy-start.6
  11.9 0.7 copy-start.7
  12.6 0.7 copy-start.8
  13.2 68.2 %copy-start.11 = (f32[8]{0:T(128)S(1)}, f32[8]{0:T(128)}, u32[]{:S(2)}) copy-start(f32[8]{0:T(128)} %param.23) | copy-start | bytes 100
  34.7 0.8 copy-start.4
  49.9 0.7 copy-start.10
  84.8 1.0 copy-start.9
Sparse Core Ops, SparseCore 0:
  90.8 32.9 reduce-scatter.1
where the time goes:
time: 146 us; the launch traced here: 145 us
  blocking collectives  42.2 us (29%)
  waiting for transfers between devices  30.1 us (21%)
  Pallas kernels  21.5 us (15%)
  local copies, waits for them, and re-layouts  17 us (12%)
  matrix products  15.9 us (11%)
  between operations  14.1 us (10%)
  other arithmetic  4.24 us (3%)
    reduce_scatter x1, waiting for transfers between devices, shards(): lax.psum_scatter(matmul(placed, own_output), 'head', scatter_dimension=0,...  30 us
    pallas_call x1, Pallas kernels, local_part(): pl.pallas_call(functools.partial(local_kernel, sizes), out_shape=[jax.Sha...  21.5 us
    all_gather x1, blocking collectives, shards(): key_piece = lax.all_gather(global_keys, 'blk', axis=0, tiled=True)  15.4 us
    all_gather x1, blocking collectives, shards(): value_piece = lax.all_gather(global_values, 'blk', axis=0, tiled=True)  14.6 us
    all_gather x1, blocking collectives, shards(): lax.all_gather(normed_two, 'head', axis=0, tiled=True)  12.2 us
    dot_general x4, matrix products, matmul(): jnp.dot(left, right, precision=PRECISE, preferred_element_type=jnp.float32)  11.4 us
    unnamed x24, local copies, waits for them, and re-layouts  9.09 us
    dot_general x1, local copies, waits for them, and re-layouts, matmul(): jnp.dot(left, right, precision=PRECISE, preferred_element_type=jnp.float32)  3.05 us
  transfers between devices with their start and end apart: 1, of which 1 were waited for; matrix products, arithmetic and copies ran while one was open for 2% of the time, Pallas kernels for 0%

commit v1 on v0

--- a/solution.py
+++ b/solution.py
@@ -10,38 +10,22 @@
 
 C0 = 256
 HEAD0 = 64
-CM = 384
 HEADS_G = 8
 HEAD_G = 64
 
 
 EPSILON = 1e-06
 FLOOR_VALUE = 0.5
-PRECISE = lax.Precision.HIGHEST
-
-
-def matmul(left, right):
-    return jnp.dot(left, right, precision=PRECISE, preferred_element_type=jnp.float32)
 
 
 def rms_scale(values, gains):
     return values * lax.rsqrt(jnp.mean(values * values, axis=-1, keepdims=True) + EPSILON) * gains
-
-
-def unit_rows(values):
-    return values * lax.rsqrt(jnp.mean(values * values, axis=-1, keepdims=True) + EPSILON)
 
 
 def floor_rows(values):
     return values * lax.rsqrt(
         jnp.maximum(jnp.mean(values * values, axis=-1, keepdims=True), FLOOR_VALUE)
     )
-
-
-def split_cells(grid_in, channels):
-    grid_rows, grid_cols = (grid_in.shape[0], grid_in.shape[1])
-    moved = grid_in.reshape(grid_rows, grid_cols, 2, 2, channels).transpose(0, 2, 1, 3, 4)
-    return moved.reshape(2 * grid_rows, 2 * grid_cols, channels)
 
 
 MESH = pl.DeviceIdType.MESH
@@ -98,10 +82,10 @@
     latent_ref,
     gain_ref,
     project_ref,
-    output_ref,
+    output_hbm,
     scale_ref,
-    merge_first_ref,
-    merge_second_ref,
+    merge_first_hbm,
+    merge_second_hbm,
     global_gain_ref,
     zero_ref,
     one_ref,
@@ -118,6 +102,10 @@
     attended_ref,
     zero_chunks,
     one_chunks,
+    output_ref,
+    merge_first_ref,
+    merge_second_ref,
+    weight_sem,
     send_sem,
     recv_sem,
 ):
@@ -135,6 +123,18 @@
         def _(device=device):
             pl.semaphore_signal(barrier, inc=1, device_id=device, device_id_type=MESH)
 
+    fetches = [
+        pltpu.make_async_copy(source, target, weight_sem.at[index])
+        for index, (source, target) in enumerate(
+            (
+                (output_hbm, output_ref),
+                (merge_first_hbm, merge_first_ref),
+                (merge_second_hbm, merge_second_ref),
+            )
+        )
+    ]
+    for fetch in fetches:
+        fetch.start()
     pl.semaphore_wait(barrier, count)
 
     sources = {-1: slice(0, HALO), 1: slice(low_row, rows)}
@@ -280,14 +280,16 @@
         return unused
 
     lax.fori_loop(0, rows // step_rows, attend, 0)
+    for fetch in fetches:
+        fetch.wait()
     zero = latent + split_dot(attended_ref[...], output_ref[...])
     zero_ref[...] = zero
     store_chunks(zero_chunks, zero)
     merged = merge_from(zero_chunks, rows, cols)
     one = split_dot(merged, merge_first_ref[...])
-    one_ref[...] = one
     store_chunks(one_chunks, one)
     merged = merge_from(one_chunks, rows // 2, cols // 2)
+    one_ref[...] = merged
     two = split_dot(merged, merge_second_ref[...])
     two_ref[...] = two
     normed_ref[...] = rms_scale(two, global_gain_ref[...])
@@ -324,17 +326,18 @@
     heads = width // HEAD0
     total = (rows + 2 * HALO) * (cols + EDGE)
     vmem = pl.BlockSpec(memory_space=pltpu.VMEM)
+    hbm = pl.BlockSpec(memory_space=pl.ANY)
     mid, coarse = merge_first.shape[1], merge_second.shape[1]
     f32, b16 = jnp.float32, jnp.bfloat16
     return pl.pallas_call(
         functools.partial(local_kernel, sizes),
         out_shape=[
             jax.ShapeDtypeStruct((rows * cols, width), f32),
-            jax.ShapeDtypeStruct((rows * cols // 4, mid), f32),
+            jax.ShapeDtypeStruct((rows * cols // 16, 4 * mid), f32),
             jax.ShapeDtypeStruct((rows * cols // 16, coarse), f32),
             jax.ShapeDtypeStruct((rows * cols // 16, coarse), f32),
         ],
-        in_specs=[vmem] * 4 + [pl.BlockSpec(memory_space=pltpu.SMEM)] + [vmem] * 3,
+        in_specs=[vmem] * 3 + [hbm, pl.BlockSpec(memory_space=pltpu.SMEM), hbm, hbm, vmem],
         out_specs=[vmem] * 4,
         scratch_shapes=[
             pltpu.VMEM((HALO, cols, width), f32),
@@ -348,6 +351,10 @@
             pltpu.VMEM((rows * cols, width), f32),
             pltpu.VMEM((width // LANES, rows * cols, LANES), f32),
             pltpu.VMEM((mid // LANES, rows * cols // 4, LANES), f32),
+            pltpu.VMEM(output.shape, f32),
+            pltpu.VMEM(merge_first.shape, f32),
+            pltpu.VMEM(merge_second.shape, f32),
+            pltpu.SemaphoreType.DMA((3,)),
             pltpu.SemaphoreType.DMA((8,)),
             pltpu.SemaphoreType.DMA((8,)),
         ],
@@ -365,6 +372,246 @@
         merge_second,
         global_gain[None],
     )
+
+
+def global_kernel(
+    sizes,
+    normed_ref,
+    two_ref,
+    one_ref,
+    zero_ref,
+    scale_ref,
+    project_hbm,
+    output_hbm,
+    split_second_hbm,
+    split_first_hbm,
+    refined_ref,
+    gather_ref,
+    proj_ref,
+    outgoing_ref,
+    incoming_ref,
+    result_ref,
+    attended_ref,
+    spread_ref,
+    project_ref,
+    output_ref,
+    split_second_ref,
+    split_first_ref,
+    weight_sem,
+    send_one,
+    recv_one,
+    send_two,
+    recv_two,
+    send_three,
+    recv_three,
+    grid,
+):
+    blocks, group = sizes
+    rows, cols = grid
+    tokens, width = normed_ref.shape
+    copies = group // HEADS_G
+    blk, me = lax.axis_index("blk"), lax.axis_index("head")
+    column = [((blk + d) % blocks, (blk + blocks - d) % blocks) for d in range(1, blocks)]
+    line = [((me + d) % group, (me + group - d) % group) for d in range(1, group)]
+
+    fetches = [
+        pltpu.make_async_copy(source, target, weight_sem.at[index])
+        for index, (source, target) in enumerate(
+            (
+                (project_hbm, project_ref),
+                (output_hbm, output_ref),
+                (split_second_hbm, split_second_ref),
+                (split_first_hbm, split_first_ref),
+            )
+        )
+    ]
+    barrier = pltpu.get_barrier_semaphore()
+    for peer, unused in column:
+        pl.semaphore_signal(barrier, inc=1, device_id=(peer, me), device_id_type=MESH)
+    for peer, unused in line:
+        pl.semaphore_signal(barrier, inc=1, device_id=(blk, peer), device_id_type=MESH)
+    for fetch in fetches:
+        fetch.start()
+    pl.semaphore_wait(barrier, blocks + group - 2)
+
+    first = [
+        pltpu.make_async_remote_copy(
+            src_ref=normed_ref,
+            dst_ref=gather_ref.at[blk],
+            send_sem=send_one.at[index],
+            recv_sem=recv_one.at[index],
+            device_id=(peer, me),
+            device_id_type=MESH,
+        )
+        for index, (peer, unused) in enumerate(column)
+    ]
+    for copy in first:
+        copy.start()
+    gather_ref[blk] = normed_ref[...]
+    fetches[0].wait()
+    for copy in first:
+        copy.wait_recv()
+    gathered = gather_ref[...].reshape(blocks * tokens, width)
+    projected = split_dot(gathered, project_ref[...])
+    proj_ref[...] = projected.reshape(blocks, tokens, projected.shape[1])
+    own = proj_ref[blk]
+    blank = jnp.zeros((tokens, HEAD_G), jnp.float32)
+    for h in range(HEADS_G):
+        start = 3 * HEAD_G * h
+        keys = floor_rows(projected[:, start + HEAD_G : start + 2 * HEAD_G])
+        values = projected[:, start + 2 * HEAD_G : start + 3 * HEAD_G]
+        queries = floor_rows(own[:, start : start + HEAD_G])
+        outgoing_ref[h, : blocks * tokens] = jnp.concatenate([keys, values], axis=1)
+        outgoing_ref[h, blocks * tokens :] = jnp.concatenate([queries, blank], axis=1)
+
+    second = [
+        pltpu.make_async_remote_copy(
+            src_ref=outgoing_ref.at[peer // copies],
+            dst_ref=incoming_ref.at[me],
+            send_sem=send_two.at[index],
+            recv_sem=recv_two.at[index],
+            device_id=(blk, peer),
+            device_id_type=MESH,
+        )
+        for index, (peer, unused) in enumerate(line)
+    ]
+    for copy in second:
+        copy.start()
+    incoming_ref[me] = outgoing_ref[me // copies]
+    for copy in second:
+        copy.wait_recv()
+
+    factor = scale_ref[0, me // copies] * (LOG2E / HEAD_G)
+    part = me % copies
+    queries = incoming_ref[pl.ds(part * HEADS_G, HEADS_G), blocks * tokens :, :HEAD_G]
+    high, low = halves(queries.reshape(HEADS_G * tokens, HEAD_G) * factor)
+    query_cat = jnp.concatenate([high, high, low, low], axis=1)
+    keyvals = incoming_ref[:, : blocks * tokens].reshape(group * blocks * tokens, 2 * HEAD_G)
+    high, low = halves(keyvals)
+    key_high, key_low = high[:, :HEAD_G], low[:, :HEAD_G]
+    value_high, value_low = high[:, HEAD_G:], low[:, HEAD_G:]
+    key_cat = jnp.concatenate([key_high, key_low, key_high, key_low], axis=1)
+    scores = lax.dot_general(
+        query_cat,
+        key_cat,
+        (((1,), (1,)), ((), ())),
+        preferred_element_type=jnp.float32,
+    )
+    weights = jnp.exp2(scores - jnp.max(scores, axis=1, keepdims=True))
+    weight_sum = jnp.sum(weights, axis=1, keepdims=True)
+    weight_high, weight_low = halves(weights)
+    wide = plain_dot(weight_high, jnp.concatenate([value_high, value_low], axis=1))
+    mixture = wide[:, :HEAD_G] + wide[:, HEAD_G:] + plain_dot(weight_low, value_high)
+    mixture = mixture / weight_sum
+    mixture = jnp.concatenate([mixture, jnp.zeros_like(mixture)], axis=1)
+    result_ref[...] = mixture.reshape(HEADS_G, tokens, 2 * HEAD_G)
+
+    head_id, my_part = me // copies, me // HEADS_G
+
+    def third(index):
+        peer = line[index][0]
+        return pltpu.make_async_remote_copy(
+            src_ref=result_ref.at[peer % HEADS_G],
+            dst_ref=attended_ref.at[head_id],
+            send_sem=send_three.at[index],
+            recv_sem=recv_three.at[index],
+            device_id=(blk, peer),
+            device_id_type=MESH,
+        )
+
+    for index, (peer, source) in enumerate(line):
+
+        @pl.when(peer // HEADS_G == part)
+        def _(index=index):
+            third(index).start()
+
+    @pl.when(my_part == part)
+    def _():
+        attended_ref[head_id] = result_ref[me % HEADS_G]
+
+    for fetch in fetches[1:]:
+        fetch.wait()
+    for index, (peer, source) in enumerate(line):
+
+        @pl.when(source % copies == my_part)
+        def _(index=index):
+            third(index).wait_recv()
+
+    attended = jnp.concatenate([attended_ref[h, :, :HEAD_G] for h in range(HEADS_G)], axis=1)
+    mixed = two_ref[...] + split_dot(attended, output_ref[...])
+    up = one_ref[...] + split_dot(mixed, split_second_ref[...])
+    mid = up.shape[1] // 4
+    up = jnp.concatenate([up[:, g * mid : (g + 1) * mid] for g in range(4)], axis=0)
+    fine = split_dot(up, split_first_ref[...])
+    cells_down, cells_across = rows // 4, cols // 4
+    chunks = spread_ref.shape[0]
+    for a in range(2):
+        for b in range(2):
+            for i in range(cells_down):
+                top = ((2 * a + b) * cells_down + i) * cells_across
+                for c in range(2):
+                    for d in range(2):
+                        at = (4 * i + 2 * a + c) * cols + 2 * b + d
+                        for chunk in range(chunks):
+                            lane = ((2 * c + d) * chunks + chunk) * LANES
+                            spread_ref[chunk, pl.ds(at, cells_across, stride=4)] = fine[
+                                top : top + cells_across, lane : lane + LANES
+                            ]
+    for chunk in range(chunks):
+        lanes = slice(chunk * LANES, (chunk + 1) * LANES)
+        refined_ref[:, lanes] = zero_ref[:, lanes] + spread_ref[chunk]
+
+    for copy in first + second:
+        copy.wait_send()
+    for index, (peer, source) in enumerate(line):
+
+        @pl.when(peer // HEADS_G == part)
+        def _(index=index):
+            third(index).wait_send()
+
+
+def global_part(grid, normed, two, one, zero, scale, project, output, split_second, split_first):
+    sizes = (lax.axis_size("blk"), lax.axis_size("head"))
+    blocks, group = sizes
+    tokens, width = normed.shape
+    vmem = pl.BlockSpec(memory_space=pltpu.VMEM)
+    hbm = pl.BlockSpec(memory_space=pl.ANY)
+    f32, dma = jnp.float32, pltpu.SemaphoreType.DMA
+    held = (blocks + 1) * tokens
+
+    def body(*refs):
+        global_kernel(sizes, *refs, grid)
+
+    return pl.pallas_call(
+        body,
+        out_shape=jax.ShapeDtypeStruct(zero.shape, f32),
+        in_specs=[vmem] * 4 + [pl.BlockSpec(memory_space=pltpu.SMEM)] + [hbm] * 4,
+        out_specs=vmem,
+        scratch_shapes=[
+            pltpu.VMEM((blocks, tokens, width), f32),
+            pltpu.VMEM((blocks, tokens, project.shape[1]), f32),
+            pltpu.VMEM((HEADS_G, held, 2 * HEAD_G), f32),
+            pltpu.VMEM((group, held, 2 * HEAD_G), f32),
+            pltpu.VMEM((HEADS_G, tokens, 2 * HEAD_G), f32),
+            pltpu.VMEM((HEADS_G, tokens, 2 * HEAD_G), f32),
+            pltpu.VMEM((zero.shape[1] // LANES, zero.shape[0], LANES), f32),
+            pltpu.VMEM(project.shape, f32),
+            pltpu.VMEM(output.shape, f32),
+            pltpu.VMEM(split_second.shape, f32),
+            pltpu.VMEM(split_first.shape, f32),
+            dma((4,)),
+            dma((blocks - 1,)),
+            dma((blocks - 1,)),
+            dma((group - 1,)),
+            dma((group - 1,)),
+            dma((group - 1,)),
+            dma((group - 1,)),
+        ],
+        compiler_params=pltpu.CompilerParams(
+            collective_id=1, has_side_effects=True, vmem_limit_bytes=48 * 2**20
+        ),
+        name="global_part",
+    )(normed, two, one, zero, scale[None], project, output, split_second, split_first)
 
 
 def shards(
@@ -393,91 +640,19 @@
         merge_second,
         global_gain,
     )
-    level_zero = level_zero.reshape(tile_rows, tile_cols, C0)
-    level_one = level_one.reshape(tile_rows // 2, tile_cols // 2, CM)
-    own_tokens = level_two.shape[0]
-    group_size = lax.axis_size("head")
-    copies = group_size // HEADS_G
-    position = lax.axis_index("head")
-    head_id = position // copies
-    part_id = position % copies
-    span = HEADS_G * own_tokens
-    own_project = lax.dynamic_slice_in_dim(global_project, head_id * 3 * HEAD_G, 3 * HEAD_G, 1)
-    projected = matmul(lax.all_gather(normed_two, "head", axis=0, tiled=True), own_project)
-    projected = projected.reshape(-1, 1, 3, HEAD_G)
-    query_part = lax.dynamic_slice_in_dim(projected[:, :, 0], part_id * span, span, 0)
-    global_queries = floor_rows(query_part)
-    global_keys = floor_rows(projected[:, :, 1])
-    global_values = projected[:, :, 2]
-    own_scale = lax.dynamic_slice_in_dim(global_scale, head_id, 1, 0)
-    factor = own_scale / HEAD_G
-    query_count = global_queries.shape[0]
-    starting = (
-        jnp.full((1, query_count), -jnp.inf, jnp.float32),
-        jnp.zeros((1, query_count), jnp.float32),
-        jnp.zeros((1, query_count, HEAD_G), jnp.float32),
-    )
-    running = starting
-    key_piece = lax.all_gather(global_keys, "blk", axis=0, tiled=True)
-    value_piece = lax.all_gather(global_values, "blk", axis=0, tiled=True)
-    piece_rows = key_piece.shape[0]
-    block_rows = math.gcd(piece_rows, 2048)
-    key_blocks = key_piece.reshape(piece_rows // block_rows, block_rows, 1, HEAD_G)
-    value_blocks = value_piece.reshape(piece_rows // block_rows, block_rows, 1, HEAD_G)
-
-    def advance(current, blocks_now):
-        key_block, value_block = blocks_now
-        best_score, weight_sum, accumulated = current
-        scores = (
-            jnp.einsum(
-                "qhd,khd->hqk",
-                global_queries,
-                key_block,
-                precision=PRECISE,
-                preferred_element_type=jnp.float32,
-            )
-            * factor[:, None, None]
-        )
-        raised_best = jnp.maximum(best_score, jnp.max(scores, axis=2))
-        rescale = jnp.exp(best_score - raised_best)
-        weights = jnp.exp(scores - raised_best[:, :, None])
-        weight_sum = weight_sum * rescale + jnp.sum(weights, axis=2)
-        accumulated = accumulated * rescale[:, :, None] + jnp.einsum(
-            "hqk,khd->hqd",
-            weights,
-            value_block,
-            precision=PRECISE,
-            preferred_element_type=jnp.float32,
-        )
-        return ((raised_best, weight_sum, accumulated), None)
-
-    running, unused = lax.scan(advance, running, (key_blocks, value_blocks))
-    best_score, weight_sum, accumulated = running
-    attention_out = (accumulated / weight_sum[:, :, None])[0]
-    placed = lax.dynamic_update_slice_in_dim(
-        jnp.zeros((group_size * own_tokens, HEAD_G), jnp.float32), attention_out, part_id * span, 0
-    )
-    own_output = lax.dynamic_slice_in_dim(global_output, head_id * HEAD_G, HEAD_G, 0)
-    mixed_global = lax.psum_scatter(
-        matmul(placed, own_output), "head", scatter_dimension=0, tiled=True
-    )
-    global_mixed = level_two + mixed_global
-    up_one = (
-        split_cells(
-            matmul(global_mixed, split_second).reshape(tile_rows // 4, tile_cols // 4, 4 * CM), CM
-        )
-        + level_one
-    )
-    refined = (
-        split_cells(
-            matmul(up_one.reshape(-1, CM), split_first).reshape(
-                tile_rows // 2, tile_cols // 2, 4 * C0
-            ),
-            C0,
-        )
-        + level_zero
-    )
-    return refined
+    refined = global_part(
+        (tile_rows, tile_cols),
+        normed_two,
+        level_two,
+        level_one,
+        level_zero,
+        global_scale,
+        global_project,
+        global_output,
+        split_second,
+        split_first,
+    )
+    return refined.reshape(tile_rows, tile_cols, C0)
 
 
 def solution(mesh):

time: 146 us -> 56.6 us (0.39)
  blocking collectives: 42.2 us -> 0 us
  waiting for transfers between devices: 30.1 us -> 0 us
  Pallas kernels: 21.5 us -> 48.9 us
  matrix products: 15.9 us -> 0 us
  between operations: 14.1 us -> 0.05 us
  local copies, waits for them, and re-layouts: 17 us -> 7.35 us
  other arithmetic: 4.24 us -> 0 us
    all_gather x3 -> x0, blocking collectives: 42.2 us -> none  [the longest x1 15.4 us: shards(): key_piece = lax.all_gather(global_keys, 'blk', axis=0, tiled=True)]
    reduce_scatter x1 -> x0, waiting for transfers between devices: 30 us -> none  [shards(): lax.psum_scatter(matmul(placed, own_output), 'head', scatter_dimension=0,...]
    pallas_call x0 -> x1, Pallas kernels: none -> 28.7 us  [global_part(): pl.pallas_call(body, out_shape=jax.ShapeDtypeStruct(zero.shape, f32), in_...]
    dot_general x6 -> x0, matrix products: 15.9 us -> none  [the longest x4 11.4 us: matmul(): jnp.dot(left, right, precision=PRECISE, preferred_element_type=jnp.float32)]
    dot_general x1 -> x0, local copies, waits for them, and re-layouts: 3.05 us -> none  [matmul(): jnp.dot(left, right, precision=PRECISE, preferred_element_type=jnp.float32)]
    add x2 -> x0, other arithmetic: 3.02 us -> none  [the longest x1 2.07 us: shards(): split_cells(matmul(up_one.reshape(-1, CM), split_first).reshape(tile_rows...]
    reshape x2 -> x0, local copies, waits for them, and re-layouts: 3.01 us -> none  [split_cells(): return moved.reshape(2 * grid_rows, 2 * grid_cols, channels)]
    unnamed x24 -> x21, local copies, waits for them, and re-layouts: 9.09 us -> 7.35 us
  transfers between devices with their start and end apart: 1 -> 0, of which waited for: 1 -> 0; matrix products, arithmetic and copies ran while one was open for 2% -> 0% of each run, Pallas kernels for 0% -> 0%
where the time goes in v1:
time: 56.6 us; the launch traced here: 56.3 us
  Pallas kernels  48.9 us (86%)
  local copies, waits for them, and re-layouts  7.35 us (13%)
    pallas_call x1, Pallas kernels, global_part(): pl.pallas_call(body, out_shape=jax.ShapeDtypeStruct(zero.shape, f32), in_...  28.7 us
    pallas_call x1, Pallas kernels, local_part(): pl.pallas_call(functools.partial(local_kernel, sizes), out_shape=[jax.Sha...  20.2 us
    unnamed x21, local copies, waits for them, and re-layouts  7.35 us

profile of v1, /device:TPU:0, one launch (start us, length us, event | category | flops | bytes accessed | tf_op | source)
XLA Modules:
  0.0 56.3 jit_solution(8982478791327561878)
XLA Ops:
  0.0 0.0 copy-start.1
  0.0 1.4 %copy-done.1 = f32[1024,384]{1,0:T(8,128)S(1)} copy-done((f32[1024,384]{1,0:T(8,128)S(1)}, f32[1024,384]{1,0:T(8,128)}, u32[]{:S(2)}) %copy-start.1) | copy-done | bytes 1572888
  1.4 0.0 copy-start.3
  1.4 1.1 %copy-done.3 = f32[256,768]{1,0:T(8,128)S(1)} copy-done((f32[256,768]{1,0:T(8,128)S(1)}, f32[256,768]{1,0:T(8,128)}, u32[]{:S(2)}) %copy-start.3) | copy-done | bytes 786456
  2.5 0.0 copy-start.4
  2.5 1.0 %copy-done.4 = f32[16,32,256]{2,1,0:T(8,128)S(1)} copy-done((f32[16,32,256]{2,1,0:T(8,128)S(1)}, f32[16,32,256]{2,1,0:T(8,128)}, u32[]{:S(2)}) %copy-start.4) | copy-done | bytes 524312
  3.6 0.0 copy-start.5
  3.6 0.9 %copy-done.5 = f32[256,256]{1,0:T(8,128)S(1)} copy-done((f32[256,256]{1,0:T(8,128)S(1)}, f32[256,256]{1,0:T(8,128)}, u32[]{:S(2)}) %copy-start.5) | copy-done | bytes 262168
  4.5 0.0 copy-start.6
  4.5 0.7 %copy-done.6 = f32[512]{0:T(512)S(1)} copy-done((f32[512]{0:T(512)S(1)}, f32[512]{0:T(512)}, u32[]{:S(2)}) %copy-start.6) | copy-done | bytes 2072
  5.2 0.0 copy-start.7
  5.2 0.7 %copy-done.7 = f32[256]{0:T(256)S(1)} copy-done((f32[256]{0:T(256)S(1)}, f32[256]{0:T(256)}, u32[]{:S(2)}) %copy-start.7) | copy-done | bytes 1048
  5.9 0.0 copy-start.8
  5.9 0.7 %copy-done.8 = f32[4]{0:T(128)S(1)} copy-done((f32[4]{0:T(128)S(1)}, f32[4]{0:T(128)}, u32[]{:S(2)}) %copy-start.8) | copy-done | bytes 40
  6.6 0.0 copy-start
  6.6 0.0 copy-start.2
  6.6 0.0 copy-start.9
  6.6 20.2 %local_part.1 = (f32[512,256]{1,0:T(8,128)S(1)}, f32[32,1536]{1,0:T(8,128)S(1)}, f32[32,512]{1,0:T(8,128)S(1)}, f32[32,512]{1,0:T(8,128)S(1)}) custom-call(f32[16,32,256]{2,1,0:T(8,128)S(1)} %copy-done.4, f32[1,256]{1,0:T(1,128)S(1)} %bitcast.7, f32[256,768]{1,0:T(8,128)S(1)} %copy-done.3, f32[256,256]{1,0:T(8,128)S(1)} %copy-done.5, f32[1,4]{1,0:T(1,128)S(1)} %bitcast.8, ...), custom_call_target="tpu_custom_call" | custom-call | tf_op jit(solution)/shard_map/local_part/pallas_call | solution.py:332
  26.7 0.0 copy-done
  26.7 0.0 copy-done.2
  26.7 0.0 copy-done.9
  26.8 28.7 %global_part.1 = f32[512,256]{1,0:T(8,128)S(1)} custom-call(f32[32,512]{1,0:T(8,128)S(1)} %get-tuple-element.9.refs_0_, f32[32,512]{1,0:T(8,128)S(1)} %get-tuple-element.10.refs_1_, f32[32,1536]{1,0:T(8,128)S(1)} %get-tuple-element.11.refs_2_, f32[512,256]{1,0:T(8,128)S(1)} %get-tuple-element.12.refs_3_, f32[1,8]{1,0:T(1,128)S(1)} %bitcast.9, ...), custom_call_target="tpu_custom_call" | custom-call | tf_op jit(solution)/shard_map/global_part/pallas_call | solution.py:585
  55.5 0.8 %copy.15 = f32[16,32,256]{2,1,0:T(8,128)} copy(f32[16,32,256]{2,1,0:T(8,128)S(1)} %bitcast.5) | data formatting | bytes 1048576
Async XLA Ops:
  0.0 1.4 %copy-start.1 = (f32[1024,384]{1,0:T(8,128)S(1)}, f32[1024,384]{1,0:T(8,128)}, u32[]{:S(2)}) copy-start(f32[1024,384]{1,0:T(8,128)} %merge_first_hbm.1) | copy-start | bytes 4718596
  1.4 1.1 %copy-start.3 = (f32[256,768]{1,0:T(8,128)S(1)}, f32[256,768]{1,0:T(8,128)}, u32[]{:S(2)}) copy-start(f32[256,768]{1,0:T(8,128)} %project_ref.1) | copy-start | bytes 2359300
  2.5 1.0 %copy-start.4 = (f32[16,32,256]{2,1,0:T(8,128)S(1)}, f32[16,32,256]{2,1,0:T(8,128)}, u32[]{:S(2)}) copy-start(f32[16,32,256]{2,1,0:T(8,128)} %latent_ref.1) | copy-start | bytes 1572868
  3.6 0.9 %copy-start.5 = (f32[256,256]{1,0:T(8,128)S(1)}, f32[256,256]{1,0:T(8,128)}, u32[]{:S(2)}) copy-start(f32[256,256]{1,0:T(8,128)} %output_hbm.1) | copy-start | bytes 786436
  4.5 0.7 %copy-start.6 = (f32[512]{0:T(512)S(1)}, f32[512]{0:T(512)}, u32[]{:S(2)}) copy-start(f32[512]{0:T(512)} %param.20) | copy-start | bytes 6148
  5.2 0.7 %copy-start.7 = (f32[256]{0:T(256)S(1)}, f32[256]{0:T(256)}, u32[]{:S(2)}) copy-start(f32[256]{0:T(256)} %param.14) | copy-start | bytes 3076
  5.9 0.7 %copy-start.8 = (f32[4]{0:T(128)S(1)}, f32[4]{0:T(128)}, u32[]{:S(2)}) copy-start(f32[4]{0:T(128)} %param.17) | copy-start | bytes 52
  6.6 20.2 %copy-start = (f32[384,1024]{1,0:T(8,128)S(1)}, f32[384,1024]{1,0:T(8,128)}, u32[]{:S(2)}) copy-start(f32[384,1024]{1,0:T(8,128)} %refs_8_.1) | copy-start | bytes 4718596
  6.6 20.2 %copy-start.2 = (f32[512,512]{1,0:T(8,128)S(1)}, f32[512,512]{1,0:T(8,128)}, u32[]{:S(2)}) copy-start(f32[512,512]{1,0:T(8,128)} %refs_6_.1) | copy-start | bytes 3145732
  6.6 20.2 %copy-start.9 = (f32[8]{0:T(128)S(1)}, f32[8]{0:T(128)}, u32[]{:S(2)}) copy-start(f32[8]{0:T(128)} %param.23) | copy-start | bytes 100

commit v2 on v1

v2 whole, which is shorter than its diff:
```python
import math

import jax
import jax.numpy as jnp
from jax import lax
from jax.experimental import pallas as pl
from jax.experimental.pallas import tpu as pltpu
from jax.sharding import PartitionSpec as P

C0 = 256
HEAD0 = 64
HEADS_G = 8
HEAD_G = 64


EPSILON = 1e-06
FLOOR_VALUE = 0.5


def rms_scale(values, gains):
    return values * lax.rsqrt(jnp.mean(values * values, axis=-1, keepdims=True) + EPSILON) * gains


def floor_rows(values):
    return values * lax.rsqrt(
        jnp.maximum(jnp.mean(values * values, axis=-1, keepdims=True), FLOOR_VALUE)
    )


MESH = pl.DeviceIdType.MESH
HALO = 3
EDGE = 8
LANES = 128
LOG2E = math.log2(math.e)
DIRECTIONS = ((-1, 0), (1, 0), (0, -1), (0, 1), (-1, -1), (-1, 1), (1, -1), (1, 1))


def halves(values):
    high = values.astype(jnp.bfloat16)
    return high, (values - high.astype(jnp.float32)).astype(jnp.bfloat16)


def plain_dot(left, right):
    return jnp.dot(left, right, preferred_element_type=jnp.float32)


def weight_dot(values, pair):
    weight_high, weight_low = pair[0][...], pair[1][...]
    high, low = halves(values)
    count = values.shape[0]
    if count > 128:
        return (
            plain_dot(low, weight_high)
            + plain_dot(high, weight_low)
            + plain_dot(high, weight_high)
        )
    both = plain_dot(jnp.concatenate([high, low], axis=0), weight_high)
    return both[count:] + plain_dot(high, weight_low) + both[:count]


def group_matrix(width, group):
    rows = lax.broadcasted_iota(jnp.int32, (width, width), 0) // group
    cols = lax.broadcasted_iota(jnp.int32, (width, width), 1) // group
    return jnp.where(rows == cols, 1.0 / group, 0.0).astype(jnp.bfloat16)


def group_mean_squares(values, group):
    high, low = halves(values * values)
    matrix = group_matrix(values.shape[1], group)
    return plain_dot(high, matrix) + plain_dot(low, matrix)


def neighbours(sizes):
    blk, head = lax.axis_index("blk"), lax.axis_index("head")
    for dz, dc in DIRECTIONS:
        row, col = blk + dz, head + dc
        back_row, back_col = blk - dz, head - dc
        there = (row >= 0) & (row < sizes[0]) & (col >= 0) & (col < sizes[1])
        back = (back_row >= 0) & (back_row < sizes[0]) & (back_col >= 0) & (back_col < sizes[1])
        yield (row, col), there, back


def local_kernel(
    sizes,
    latent_hbm,
    latent_ref,
    gain_ref,
    scale_ref,
    global_gain_ref,
    prepare,
    fetch_small,
    pairs,
    one_ref,
    two_ref,
    normed_ref,
    up_ref,
    down_ref,
    left_ref,
    right_ref,
    query_ref,
    key_ref,
    high_ref,
    low_ref,
    attended_ref,
    zero_chunks,
    one_chunks,
    send_sem,
    recv_sem,
):
    rows, cols, width = latent_ref.shape
    heads = width // HEAD0
    span = cols + EDGE
    low_row, low_col = rows - HALO, cols - EDGE
    blk, head = lax.axis_index("blk"), lax.axis_index("head")
    sources = {-1: slice(0, HALO), 1: slice(low_row, rows)}
    corner_rows = {-1: slice(rows + HALO, rows + 2 * HALO), 1: slice(0, HALO)}
    columns = {-1: slice(0, EDGE), 1: slice(low_col, cols)}

    def copy_of(index, device):
        dz, dc = DIRECTIONS[index]
        if dc == 0:
            source = latent_hbm.at[sources[dz]]
            target = down_ref if dz < 0 else up_ref
        else:
            side = right_ref if dc < 0 else left_ref
            if dz == 0:
                source = latent_hbm.at[:, columns[dc]]
                target = side.at[HALO : HALO + rows]
            else:
                source = latent_hbm.at[sources[dz], columns[dc]]
                target = side.at[corner_rows[dz]]
        return pltpu.make_async_remote_copy(
            src_ref=source,
            dst_ref=target,
            send_sem=send_sem.at[index],
            recv_sem=recv_sem.at[index],
            device_id=device,
            device_id_type=MESH,
        )

    for index, (device, there, back) in enumerate(neighbours(sizes)):

        @pl.when(there)
        def _(index=index, device=device):
            copy_of(index, device).start()

    fetch_small()
    prepare(0)
    gain = gain_ref[...]
    head_factor = jnp.concatenate(
        [jnp.broadcast_to(scale_ref[:, h : h + 1], (1, HEAD0)) for h in range(heads)],
        axis=1,
    )
    head_factor = head_factor * (LOG2E / HEAD0)
    latent = latent_ref[...].reshape(rows * cols, width)
    normed = rms_scale(latent, gain)
    queries = weight_dot(normed, [ref.at[:, :width] for ref in pairs[0]])
    queries = queries * lax.rsqrt(group_mean_squares(queries, HEAD0) + EPSILON) * head_factor
    high, low = halves(queries)
    for h in range(heads):
        a, b = high[:, h * HEAD0 : (h + 1) * HEAD0], low[:, h * HEAD0 : (h + 1) * HEAD0]
        query_ref[h] = jnp.concatenate([a, a, b, b], axis=1)
    for index in (1, 2, 3):
        prepare(index)

    for index, (device, there, back) in enumerate(neighbours(sizes)):

        @pl.when(back)
        def _(index=index, device=device):
            copy_of(index, device).wait_recv()

        @pl.when(there)
        def _(index=index, device=device):
            copy_of(index, device).wait_send()

    has_up, has_down = blk > 0, blk < sizes[0] - 1
    has_left, has_right = head > 0, head < sizes[1] - 1
    middle = jnp.concatenate(
        [
            jnp.where(has_up, up_ref[...], 0.0),
            latent_ref[...],
            jnp.where(has_down, down_ref[...], 0.0),
        ],
        axis=0,
    )
    shape = (rows + 2 * HALO, EDGE, width)
    spot = lax.broadcasted_iota(jnp.int32, shape, 1)
    layer = lax.broadcasted_iota(jnp.int32, shape, 0)
    row_there = (has_up | (layer >= HALO)) & (has_down | (layer < rows + HALO))
    side = jnp.where(
        (spot < HALO) & has_right & row_there,
        right_ref[...],
        jnp.where((spot >= EDGE - HALO) & has_left & row_there, left_ref[...], 0.0),
    )
    padded_rows = rows + 2 * HALO
    total = padded_rows * span
    everything = jnp.concatenate([middle, side], axis=1).reshape(total, width)
    keyvals = weight_dot(
        rms_scale(everything, gain), [ref.at[:, width:] for ref in pairs[0]]
    )
    keys = keyvals[:, :width]
    keys = keys * lax.rsqrt(group_mean_squares(keys, HEAD0) + EPSILON)
    high, low = halves(keys)
    value_high, value_low = halves(keyvals[:, width:])
    for h in range(heads):
        part = slice(h * HEAD0, (h + 1) * HEAD0)
        a, b = high[:, part], low[:, part]
        key_ref[h] = jnp.concatenate([a, b, a, b], axis=1)
        high_ref[h] = jnp.concatenate([value_high[:, part], value_low[:, part]], axis=1)
        low_ref[h] = value_high[:, part]

    step_rows = 4
    block = step_rows * cols
    reach = (step_rows + 2 * HALO) * span
    query_at = lax.broadcasted_iota(jnp.int32, (block, 1), 0)
    key_at = lax.broadcasted_iota(jnp.int32, (1, reach), 1)
    query_row, query_col = query_at // cols, query_at % cols
    key_row, place = key_at // span, key_at % span
    key_col = jnp.where(
        place < cols + HALO,
        place,
        jnp.where(place >= span - HALO, place - span, -4 * span),
    )
    col_here = (
        (key_col + head * cols >= 0)
        & (key_col + head * cols < sizes[1] * cols)
    )
    key_col = jnp.where(col_here, key_col, -4 * span)
    row_gap, col_gap = key_row - query_row, key_col - query_col
    near = (row_gap >= 0) & (row_gap <= 2 * HALO) & (col_gap >= -HALO) & (col_gap <= HALO)
    near_bias = jnp.where(near, 0.0, -1e30)

    def attend(step, unused):
        grid_row = blk * rows + step * step_rows - HALO + key_row
        bias = near_bias + jnp.where(
            (grid_row >= 0) & (grid_row < sizes[0] * rows), 0.0, -1e30
        )
        queries_at = pl.ds(pl.multiple_of(step * block, block), block)
        keys_at = pl.ds(pl.multiple_of(step * step_rows * span, step_rows * span), reach)
        parts = []
        for h in range(heads):
            scores = (
                lax.dot_general(
                    query_ref[h, queries_at],
                    key_ref[h, keys_at],
                    (((1,), (1,)), ((), ())),
                    preferred_element_type=jnp.float32,
                )
                + bias
            )
            weights = jnp.exp2(scores - jnp.max(scores, axis=1, keepdims=True))
            weight_sum = jnp.sum(weights, axis=1, keepdims=True)
            weight_high, weight_low = halves(weights)
            wide = plain_dot(weight_high, high_ref[h, keys_at])
            mixture = (
                wide[:, :HEAD0]
                + wide[:, HEAD0:]
                + plain_dot(weight_low, low_ref[h, keys_at])
            )
            parts.append(mixture / weight_sum)
        attended_ref[queries_at] = jnp.concatenate(parts, axis=1)
        return unused

    lax.fori_loop(0, rows // step_rows, attend, 0)
    zero = latent + weight_dot(attended_ref[...], pairs[1])
    store_chunks(zero_chunks, zero)
    merged = merge_from(zero_chunks, rows, cols)
    one = weight_dot(merged, pairs[2])
    store_chunks(one_chunks, one)
    merged = merge_from(one_chunks, rows // 2, cols // 2)
    one_ref[...] = merged
    two = weight_dot(merged, pairs[3])
    two_ref[...] = two
    normed_ref[...] = rms_scale(two, global_gain_ref[...])


def store_chunks(ref, values):
    for chunk in range(ref.shape[0]):
        ref[chunk] = values[:, chunk * LANES : (chunk + 1) * LANES]


def merge_from(ref, rows, cols):
    cells, width = rows * cols, ref.shape[0] * LANES
    evens, odds = (
        jnp.concatenate(
            [
                ref[chunk, pl.ds(start, cells // 2, stride=2)]
                for chunk in range(ref.shape[0])
            ],
            axis=1,
        ).reshape(rows // 2, 2, cols // 2, width)
        for start in (0, 1)
    )
    pieces = [
        source[:, which].reshape(cells // 4, width)
        for which in (0, 1)
        for source in (evens, odds)
    ]
    return jnp.concatenate(pieces, axis=1)


def global_kernel(
    sizes,
    grid,
    scale_ref,
    prepare,
    pairs,
    one_ref,
    two_ref,
    normed_ref,
    zero_chunks,
    refined_ref,
    gather_ref,
    outgoing_ref,
    incoming_ref,
    result_ref,
    attended_ref,
    spread_ref,
    send_one,
    recv_one,
    send_two,
    recv_two,
    send_three,
    recv_three,
):
    blocks, group = sizes
    rows, cols = grid
    tokens, width = normed_ref.shape
    copies = group // HEADS_G
    blk, me = lax.axis_index("blk"), lax.axis_index("head")
    column = [((blk + d) % blocks, (blk + blocks - d) % blocks) for d in range(1, blocks)]
    line = [((me + d) % group, (me + group - d) % group) for d in range(1, group)]

    first = [
        pltpu.make_async_remote_copy(
            src_ref=normed_ref,
            dst_ref=gather_ref.at[index],
            send_sem=send_one.at[index],
            recv_sem=recv_one.at[index],
            device_id=(peer, me),
            device_id_type=MESH,
        )
        for index, (peer, unused) in enumerate(column)
    ]
    for copy in first:
        copy.start()
    prepare(4)
    own_rows = 2 * tokens
    stages = (slice(0, own_rows), slice(own_rows, own_rows + (blocks - 1) * tokens))

    def second(stage, index):
        peer = line[index][0]
        return pltpu.make_async_remote_copy(
            src_ref=outgoing_ref.at[peer // copies, stages[stage]],
            dst_ref=incoming_ref.at[me, stages[stage]],
            send_sem=send_two.at[stage, index],
            recv_sem=recv_two.at[stage, index],
            device_id=(blk, peer),
            device_id_type=MESH,
        )

    def key_values(projected, h):
        start = 3 * HEAD_G * h
        keys = floor_rows(projected[:, start + HEAD_G : start + 2 * HEAD_G])
        values = projected[:, start + 2 * HEAD_G : start + 3 * HEAD_G]
        return jnp.concatenate([keys, values], axis=1)

    own = weight_dot(normed_ref[...], pairs[4])
    blank = jnp.zeros((tokens, HEAD_G), jnp.float32)
    for h in range(HEADS_G):
        start = 3 * HEAD_G * h
        queries = floor_rows(own[:, start : start + HEAD_G])
        outgoing_ref[h, :tokens] = key_values(own, h)
        outgoing_ref[h, tokens:own_rows] = jnp.concatenate([queries, blank], axis=1)
    for index in range(group - 1):
        second(0, index).start()
    for index in (5, 6, 7):
        prepare(index)
    for copy in first:
        copy.wait_recv()
    gathered = gather_ref[...].reshape((blocks - 1) * tokens, width)
    projected = weight_dot(gathered, pairs[4])
    for h in range(HEADS_G):
        outgoing_ref[h, own_rows:] = key_values(projected, h)
    for index in range(group - 1):
        second(1, index).start()
    incoming_ref[me] = outgoing_ref[me // copies]
    for index in range(group - 1):
        for stage in range(2):
            second(stage, index).wait_recv()

    lane_of = lax.broadcasted_iota(jnp.int32, scale_ref.shape, 1)
    own_scale = jnp.where(lane_of == me // copies, scale_ref[...], 0.0)
    factor = jnp.sum(own_scale, axis=1, keepdims=True) * (LOG2E / HEAD_G)
    part = me % copies
    queries = incoming_ref[pl.ds(part * HEADS_G, HEADS_G), tokens:own_rows, :HEAD_G]
    high, low = halves(queries.reshape(HEADS_G * tokens, HEAD_G) * factor)
    query_cat = jnp.concatenate([high, high, low, low], axis=1)
    keyvals = jnp.concatenate([incoming_ref[:, :tokens], incoming_ref[:, own_rows:]], axis=1)
    keyvals = keyvals.reshape(group * blocks * tokens, 2 * HEAD_G)
    high, low = halves(keyvals)
    key_high, key_low = high[:, :HEAD_G], low[:, :HEAD_G]
    value_high, value_low = high[:, HEAD_G:], low[:, HEAD_G:]
    key_cat = jnp.concatenate([key_high, key_low, key_high, key_low], axis=1)
    scores = lax.dot_general(
        query_cat,
        key_cat,
        (((1,), (1,)), ((), ())),
        preferred_element_type=jnp.float32,
    )
    weights = jnp.exp2(scores - jnp.max(scores, axis=1, keepdims=True))
    weight_sum = jnp.sum(weights, axis=1, keepdims=True)
    weight_high, weight_low = halves(weights)
    wide = plain_dot(weight_high, jnp.concatenate([value_high, value_low], axis=1))
    mixture = wide[:, :HEAD_G] + wide[:, HEAD_G:] + plain_dot(weight_low, value_high)
    mixture = mixture / weight_sum
    mixture = jnp.concatenate([mixture, jnp.zeros_like(mixture)], axis=1)
    result_ref[...] = mixture.reshape(HEADS_G, tokens, 2 * HEAD_G)

    head_id, my_part = me // copies, me // HEADS_G

    def third(index):
        peer = line[index][0]
        return pltpu.make_async_remote_copy(
            src_ref=result_ref.at[peer % HEADS_G],
            dst_ref=attended_ref.at[head_id],
            send_sem=send_three.at[index],
            recv_sem=recv_three.at[index],
            device_id=(blk, peer),
            device_id_type=MESH,
        )

    for index, (peer, source) in enumerate(line):

        @pl.when(peer // HEADS_G == part)
        def _(index=index):
            third(index).start()

    @pl.when(my_part == part)
    def _():
        attended_ref[head_id] = result_ref[me % HEADS_G]

    for index, (peer, source) in enumerate(line):

        @pl.when(source % copies == my_part)
        def _(index=index):
            third(index).wait_recv()

    attended = jnp.concatenate([attended_ref[h, :, :HEAD_G] for h in range(HEADS_G)], axis=1)
    mixed = two_ref[...] + weight_dot(attended, pairs[5])
    up = one_ref[...] + weight_dot(mixed, pairs[6])
    mid = up.shape[1] // 4
    up = jnp.concatenate([up[:, g * mid : (g + 1) * mid] for g in range(4)], axis=0)
    fine = weight_dot(up, pairs[7])
    cells_down, cells_across = rows // 4, cols // 4
    chunks = spread_ref.shape[0]
    for a in range(2):
        for b in range(2):
            for i in range(cells_down):
                top = ((2 * a + b) * cells_down + i) * cells_across
                for c in range(2):
                    for d in range(2):
                        at = (4 * i + 2 * a + c) * cols + 2 * b + d
                        for chunk in range(chunks):
                            lane = ((2 * c + d) * chunks + chunk) * LANES
                            spread_ref[chunk, pl.ds(at, cells_across, stride=4)] = fine[
                                top : top + cells_across, lane : lane + LANES
                            ]
    for chunk in range(chunks):
        lanes = slice(chunk * LANES, (chunk + 1) * LANES)
        refined_ref[:, lanes] = zero_chunks[chunk] + spread_ref[chunk]

    for copy in first:
        copy.wait_send()
    for index in range(group - 1):
        for stage in range(2):
            second(stage, index).wait_send()
    for index, (peer, source) in enumerate(line):

        @pl.when(peer // HEADS_G == part)
        def _(index=index):
            third(index).wait_send()


SMALL = (1, 4, 7, 10)
LARGE = (2, 3, 5, 6, 8, 9, 11, 12)


def whole_kernel(sizes, inputs, output, staged, highs, lows, kept, local_scratch, global_scratch, sems):
    input_sem, send_sem, recv_sem, *global_sems = sems
    rows, cols = inputs[0].shape[:2]
    barrier = pltpu.get_barrier_semaphore()
    blk, head = lax.axis_index("blk"), lax.axis_index("head")

    fetches = [
        pltpu.make_async_copy(source, target, input_sem.at[index])
        for index, (source, target) in enumerate(zip(inputs, staged))
    ]
    count = jnp.int32(sizes[0] + sizes[1] - 2)
    for d in range(1, sizes[0]):
        peer = (blk + d) % sizes[0]
        pl.semaphore_signal(barrier, inc=1, device_id=(peer, head), device_id_type=MESH)
    for d in range(1, sizes[1]):
        peer = (head + d) % sizes[1]
        pl.semaphore_signal(barrier, inc=1, device_id=(blk, peer), device_id_type=MESH)
    for (dz, dc), (device, there, back) in zip(DIRECTIONS, neighbours(sizes)):
        if dz and dc:
            count = count + there.astype(jnp.int32)

            @pl.when(there)
            def _(device=device):
                pl.semaphore_signal(barrier, inc=1, device_id=device, device_id_type=MESH)

    for fetch in fetches:
        fetch.start()
    pl.semaphore_wait(barrier, count)

    def prepare(which):
        index = LARGE[which]
        fetches[index].wait()
        highs[which][...], lows[which][...] = halves(staged[index][...])

    def fetch_small():
        for index in (0,) + SMALL:
            fetches[index].wait()

    pairs = list(zip(highs, lows))
    one_ref, two_ref, normed_ref = kept
    local_kernel(
        sizes,
        inputs[0],
        staged[0],
        staged[1],
        staged[4],
        staged[7],
        prepare,
        fetch_small,
        pairs,
        one_ref,
        two_ref,
        normed_ref,
        *local_scratch,
        send_sem,
        recv_sem,
    )
    global_kernel(
        sizes,
        (rows, cols),
        staged[10],
        prepare,
        pairs,
        one_ref,
        two_ref,
        normed_ref,
        local_scratch[-2],
        output,
        *global_scratch,
        *global_sems,
    )


def shards(*arrays):
    arrays = [array[None] if array.ndim == 1 else array for array in arrays]
    rows, cols, width = arrays[0].shape
    sizes = (lax.axis_size("blk"), lax.axis_size("head"))
    blocks, group = sizes
    heads = width // HEAD0
    total = (rows + 2 * HALO) * (cols + EDGE)
    mid, coarse = arrays[5].shape[1], arrays[6].shape[1]
    tokens = rows * cols // 16
    held = (blocks + 1) * tokens
    f32, b16, dma = jnp.float32, jnp.bfloat16, pltpu.SemaphoreType.DMA
    weights = [pltpu.VMEM(arrays[index].shape, b16) for index in LARGE]
    scratch = (
        [pltpu.VMEM(array.shape, f32) for array in arrays],
        weights,
        weights,
        [
            pltpu.VMEM((tokens, 4 * mid), f32),
            pltpu.VMEM((tokens, coarse), f32),
            pltpu.VMEM((tokens, coarse), f32),
        ],
        [
            pltpu.VMEM((HALO, cols, width), f32),
            pltpu.VMEM((HALO, cols, width), f32),
            pltpu.VMEM((rows + 2 * HALO, EDGE, width), f32),
            pltpu.VMEM((rows + 2 * HALO, EDGE, width), f32),
            pltpu.VMEM((heads, rows * cols, 4 * HEAD0), b16),
            pltpu.VMEM((heads, total, 4 * HEAD0), b16),
            pltpu.VMEM((heads, total, 2 * HEAD0), b16),
            pltpu.VMEM((heads, total, HEAD0), b16),
            pltpu.VMEM((rows * cols, width), f32),
            pltpu.VMEM((width // LANES, rows * cols, LANES), f32),
            pltpu.VMEM((mid // LANES, rows * cols // 4, LANES), f32),
        ],
        [
            pltpu.VMEM((blocks - 1, tokens, coarse), f32),
            pltpu.VMEM((HEADS_G, held, 2 * HEAD_G), f32),
            pltpu.VMEM((group, held, 2 * HEAD_G), f32),
            pltpu.VMEM((HEADS_G, tokens, 2 * HEAD_G), f32),
            pltpu.VMEM((HEADS_G, tokens, 2 * HEAD_G), f32),
            pltpu.VMEM((width // LANES, rows * cols, LANES), f32),
        ],
        [
            dma((len(arrays),)),
            dma((8,)),
            dma((8,)),
            dma((blocks - 1,)),
            dma((blocks - 1,)),
            dma((2, group - 1)),
            dma((2, group - 1)),
            dma((group - 1,)),
            dma((group - 1,)),
        ],
    )

    def body(*refs):
        refs = list(refs)
        inputs, output, rest = refs[: len(arrays)], refs[len(arrays)], refs[len(arrays) + 1 :]
        parts = []
        for shapes in scratch:
            parts.append(rest[: len(shapes)])
            rest = rest[len(shapes) :]
        whole_kernel(sizes, inputs, output, *parts)

    refined = pl.pallas_call(
        body,
        out_shape=jax.ShapeDtypeStruct((rows * cols, width), f32),
        in_specs=[pl.BlockSpec(memory_space=pl.ANY)] * len(arrays),
        out_specs=pl.BlockSpec(memory_space=pltpu.VMEM),
        scratch_shapes=[shape for shapes in scratch for shape in shapes],
        compiler_params=pltpu.CompilerParams(
            collective_id=0, has_side_effects=True, vmem_limit_bytes=60 * 2**20
        ),
        name="window",
    )(*arrays)
    return refined.reshape(rows, cols, width)


def solution(mesh):
    in_specs = (P("blk", "head", None), P(), P(), P(), P(), P(), P(), P(), P(), P(), P(), P(), P())
    out_specs = P("blk", "head", None)
    return jax.shard_map(shards, mesh=mesh, in_specs=in_specs, out_specs=out_specs, check_vma=False)
```

time: 56.6 us -> 44.7 us (0.79)
  Pallas kernels: 48.9 us -> 42.7 us
  local copies, waits for them, and re-layouts: 7.35 us -> 1.88 us
    pallas_call x2 -> x1, Pallas kernels: 48.9 us -> 42.7 us  [shards(): pl.pallas_call(body, out_shape=jax.ShapeDtypeStruct((rows * cols, width),...]
    unnamed x21 -> x1, local copies, waits for them, and re-layouts: 7.35 us -> 1.88 us
where the time goes in v2:
time: 44.7 us; the launch traced here: 44.6 us
  Pallas kernels  42.7 us (96%)
  local copies, waits for them, and re-layouts  1.88 us (4%)
    pallas_call x1, Pallas kernels, shards(): pl.pallas_call(body, out_shape=jax.ShapeDtypeStruct((rows * cols, width),...  42.7 us
    unnamed x1, local copies, waits for them, and re-layouts  1.88 us

profile of v2, /device:TPU:0, one launch (start us, length us, event | category | flops | bytes accessed | tf_op | source)
XLA Modules:
  0.0 44.6 jit_solution(11453702504693888704)
XLA Ops:
  0.0 42.7 %window.1 = f32[512,256]{1,0:T(8,128)} custom-call(f32[16,32,256]{2,1,0:T(8,128)} %refs_0_.1, f32[1,256]{1,0:T(1,128)} %bitcast.7, f32[256,768]{1,0:T(8,128)} %refs_2_.1, f32[256,256]{1,0:T(8,128)} %refs_3_.1, f32[1,4]{1,0:T(1,128)} %bitcast.8, f32[1024,384]{1,0:T(8,128)} %refs_5_.1, f32[1536,512]{1,0:T(8,128)} %refs_6_.1, f32[1,512]{1,0:T(1,128)} %bitcast.6, ...), custom_call_target="tpu_custom_call" | custom-call | tf_op jit(solution)/shard_map/window/pallas_call | solution.py:626
  42.7 1.9 %copy.15 = f32[16,32,256]{2,1,0:T(8,128)} copy(f32[16,32,256]{2,1,0:T(8,128)} %bitcast.5) | data formatting | bytes 1048576

commit v3 on v2

--- a/solution.py
+++ b/solution.py
@@ -374,8 +374,6 @@
         outgoing_ref[h, tokens:own_rows] = jnp.concatenate([queries, blank], axis=1)
     for index in range(group - 1):
         second(0, index).start()
-    for index in (5, 6, 7):
-        prepare(index)
     for copy in first:
         copy.wait_recv()
     gathered = gather_ref[...].reshape((blocks - 1) * tokens, width)
@@ -385,6 +383,8 @@
     for index in range(group - 1):
         second(1, index).start()
     incoming_ref[me] = outgoing_ref[me // copies]
+    for index in (5, 6, 7):
+        prepare(index)
     for index in range(group - 1):
         for stage in range(2):
             second(stage, index).wait_recv()

time: 44.7 us -> 44.7 us (level)
  no operation moved by 1% of the time
where the time goes in v3:
time: 44.7 us; the launch traced here: 44.5 us
  Pallas kernels  42.7 us (96%)
  local copies, waits for them, and re-layouts  1.88 us (4%)
    pallas_call x1, Pallas kernels, shards(): pl.pallas_call(body, out_shape=jax.ShapeDtypeStruct((rows * cols, width),...  42.7 us
    unnamed x1, local copies, waits for them, and re-layouts  1.88 us

profile of v3, /device:TPU:0, one launch (start us, length us, event | category | flops | bytes accessed | tf_op | source)
XLA Modules:
  0.0 44.5 jit_solution(8669312559984013915)
XLA Ops:
  0.0 42.7 %window.1 = f32[512,256]{1,0:T(8,128)} custom-call(f32[16,32,256]{2,1,0:T(8,128)} %refs_0_.1, f32[1,256]{1,0:T(1,128)} %bitcast.7, f32[256,768]{1,0:T(8,128)} %refs_2_.1, f32[256,256]{1,0:T(8,128)} %refs_3_.1, f32[1,4]{1,0:T(1,128)} %bitcast.8, f32[1024,384]{1,0:T(8,128)} %refs_5_.1, f32[1536,512]{1,0:T(8,128)} %refs_6_.1, f32[1,512]{1,0:T(1,128)} %bitcast.6, ...), custom_call_target="tpu_custom_call" | custom-call | tf_op jit(solution)/shard_map/window/pallas_call | solution.py:626
  42.7 1.9 %copy.15 = f32[16,32,256]{2,1,0:T(8,128)} copy(f32[16,32,256]{2,1,0:T(8,128)} %bitcast.5) | data formatting | bytes 1048576
